TPU v7x, 32 devices: a whole 2x2x4 slice. The times are simulated.
32 devices in a mesh: tile: 8 (over y, x, core), col: 4 (over z).
Axes of the slice: x: 2, y: 2, z: 4, core: 2. Of those that a mesh axis runs over, the one named last changes fastest.
Arguments:
- u_velocity: float32 [4096, 2048], P('tile', 'col'), may hold values from -12 to 12
- v_velocity: float32 [4096, 2048], P('tile', 'col'), may hold values from -12 to 12
- ocean_mask: int32 [32, 16], P('tile', 'col'), may hold values from 0 to 1, as said below
- tile_owner: int32 [32, 16], P('tile', 'col'), may hold values from 0 to 7, as said below
- lower_edge_quarter_turns: int32 [8], replicated, may hold values from 0 to 3
Outputs:
- library: float32 [8, 4, 16, 16, 1024], P('tile', 'col')
- gram: float32 [16, 16], replicated
Inputs may be any that keep to these rules, and one draw needn't show every extreme that they name: `ocean_mask`: in every column of devices (4 x 4 tile blocks), at least one device has only ocean tiles. `tile_owner`: among the ocean tiles of one device at most 2 share an owner; the ocean tiles of one column of devices are spread over its 8 owners so that the owners' counts differ by at most one. Land tiles carry an owner that is not used.
All inputs are finite; a program needn't handle non-finite values.
Results may differ from a plain program's by a relative error of at most 0.00014.
Values sent between devices are 32-bit elements; how exact they have to be, the bound alone decides.
A program may use at most 192 MiB of HBM per device.

v0:
```python
import functools

import jax
import jax.numpy as jnp
from jax import lax
from jax.experimental import pallas as pl
from jax.experimental.pallas import tpu as pltpu
from jax.sharding import PartitionSpec as P

PASSES = 8
KAPPA = 0.2
TERMS = 16
LANES = 128
HALO = 16
MARGIN = 8
STEP = 112
PAIR = 2
MESH = pl.DeviceIdType.MESH


def lanes_of(shape):
    return lax.broadcasted_iota(jnp.int32, shape, len(shape) - 1)


def turn(first, second, turns):
    cosine = jnp.where(turns == 0, 1.0, jnp.where(turns == 2, -1.0, 0.0)).astype(jnp.float32)
    sine = jnp.where(turns == 1, 1.0, jnp.where(turns == 3, -1.0, 0.0)).astype(jnp.float32)
    return cosine * first - sine * second, sine * first + cosine * second


def make_terms(u_part, v_part, vort, strain, stretch):
    return [
        u_part, v_part, vort, strain, stretch, vort * vort, vort * strain, vort * stretch,
        strain * strain, stretch * stretch, strain * stretch, u_part * vort, v_part * vort,
        u_part * strain, v_part * stretch, u_part * v_part,
    ]


def kernel(n_tile, n_col, grid_x, grid_y, u_ref, v_ref, mask_ref, owner_ref, turns_ref,
           library_ref, gram_ref, strip_a, strip_b, weights, row_sums, centre, across, fields,
           tiles, terms, out_tiles, in_tiles, block_terms, pack, in_cols, in_rows, in_corners,
           gram_out, gram_in, gram_out2, gram_in2, pick, kept,
           halo_send, halo_recv, all_send, all_recv, sum_send, sum_recv, sum2_send, sum2_recv,
           own_sem):
    t = lax.axis_index("tile")
    c = lax.axis_index("col")
    up, down = lax.rem(t + n_tile - 1, n_tile), lax.rem(t + 1, n_tile)
    left, right = lax.rem(c + n_col - 1, n_col), lax.rem(c + 1, n_col)
    rows, cols = u_ref.shape
    count = grid_x * grid_y
    slots = count // n_tile
    inputs = (u_ref, v_ref)
    last = cols - LANES

    tile_peers = [(lax.rem(t + d, n_tile), c) for d in range(1, n_tile)]
    col_peers = [(t, lax.rem(c + d, n_col)) for d in range(1, n_col)]
    corners = [(up, left), (up, right), (down, left), (down, right)]
    barrier = pltpu.get_barrier_semaphore()
    everyone = tile_peers + col_peers + corners
    for peer in everyone:
        pl.semaphore_signal(barrier, inc=1, device_id=peer, device_id_type=MESH)

    group = rows // 8
    lane = lanes_of((group, LANES))
    for comp in range(PAIR):
        first = jnp.zeros((group, LANES), jnp.float32)
        final = jnp.zeros((group, LANES), jnp.float32)
        for j in range(8):
            here = (lane >= HALO * j) & (lane < HALO * (j + 1))
            block = inputs[comp][j * group:(j + 1) * group, :LANES]
            first = jnp.where(here, pltpu.roll(block, HALO * j, 1) if j else block, first)
            block = inputs[comp][j * group:(j + 1) * group, last:]
            final = jnp.where(here, pltpu.roll(block, HALO * (j + 1), 1) if j < 7 else block, final)
        pack[0, comp] = first
        pack[1, comp] = final

    pl.semaphore_wait(barrier, len(everyone))

    copies = []

    def send(src, dst, peer):
        k = len(copies)
        copy = pltpu.make_async_remote_copy(
            src_ref=src, dst_ref=dst, send_sem=halo_send.at[k], recv_sem=halo_recv.at[k],
            device_id=peer, device_id_type=MESH)
        copy.start()
        copies.append(copy)

    send(pack.at[1], in_cols.at[0], (t, right))
    send(pack.at[0], in_cols.at[1], (t, left))
    for comp in range(PAIR):
        send(inputs[comp].at[pl.ds(rows - HALO, HALO), :], in_rows.at[0, comp], (down, c))
        send(inputs[comp].at[pl.ds(0, HALO), :], in_rows.at[1, comp], (up, c))
    for comp in range(PAIR):
        low = inputs[comp].at[pl.ds(rows - HALO, HALO), :]
        high = inputs[comp].at[pl.ds(0, HALO), :]
        send(low.at[:, pl.ds(last, LANES)], in_corners.at[0, comp], (down, right))
        send(low.at[:, pl.ds(0, LANES)], in_corners.at[1, comp], (down, left))
        send(high.at[:, pl.ds(last, LANES)], in_corners.at[2, comp], (up, right))
        send(high.at[:, pl.ds(0, LANES)], in_corners.at[3, comp], (up, left))

    for o in range(n_tile):
        seen = jnp.int32(0)
        chosen = [jnp.int32(0)] * slots
        for h in range(count):
            hit = (mask_ref[h // grid_y, h % grid_y] == 1) & (owner_ref[h // grid_y, h % grid_y] == o)
            for p in range(slots):
                chosen[p] = jnp.where(hit & (seen == p), h, chosen[p])
            seen = seen + jnp.where(hit, 1, 0)
        for p in range(slots):
            pick[o * slots + p] = chosen[p]
            kept[o * slots + p] = jnp.where(seen > p, 1.0, 0.0).astype(jnp.float32)

    strips = strip_a.shape[0] // PAIR
    for s in range(strips):
        spot = lax.broadcasted_iota(jnp.int32, (LANES, 2 * LANES), 0)
        cell = lax.broadcasted_iota(jnp.int32, (LANES, 2 * LANES), 1)
        from_col = (spot + (s * STEP - HALO)) >> 2
        valid = (spot >= PASSES) & (spot < LANES - PASSES)
        low_half = cell < LANES
        target = jnp.where(low_half, cell, cell - LANES)
        plus = jnp.where(low_half, target, target + 1) == from_col
        minus = (jnp.logical_not(low_half)) & (target - 1 == from_col)
        value = jnp.where(plus, 1.0, jnp.where(minus, -1.0, 0.0))
        weights[s * LANES:(s + 1) * LANES, :] = jnp.where(valid, value, 0.0).astype(jnp.bfloat16)
    row_sums[...] = jnp.zeros(row_sums.shape, jnp.float32)
    for job in range(PAIR * strips):
        edge = jnp.zeros((MARGIN, LANES), jnp.float32)
        total = strip_a.shape[1]
        strip_a[job, 0:MARGIN, :] = edge
        strip_a[job, total - MARGIN:total, :] = edge
        strip_b[job, 0:MARGIN, :] = edge
        strip_b[job, total - MARGIN:total, :] = edge

    def split_strips(x, height):
        lane = lanes_of((height, LANES))
        out = []
        for s in range(1, strips - 1):
            shift = HALO * (s + 1)
            out.append(jnp.where(lane < shift, pltpu.roll(x[s - 1], shift, 1), pltpu.roll(x[s], shift, 1)))
        return out

    def outer_strips(x0, x3, before, after, height):
        lane = lanes_of((height, LANES))
        return (jnp.where(lane < HALO, before, pltpu.roll(x0, HALO, 1)),
                jnp.where(lane < HALO * strips, pltpu.roll(x3, HALO * strips, 1), after))

    top = MARGIN + HALO
    chunk = 32
    for comp in range(PAIR):
        for r in range(0, rows, chunk):
            x = [inputs[comp][r:r + chunk, k * LANES:(k + 1) * LANES] for k in range(cols // LANES)]
            for s, value in enumerate(split_strips(x, chunk)):
                strip_a[comp * strips + s + 1, top + r:top + r + chunk, :] = value

    for copy in copies:
        copy.wait()

    for comp in range(PAIR):
        for j in range(8):
            before_all = in_cols[0, comp]
            after_all = in_cols[1, comp]
            before_all = pltpu.roll(before_all, LANES - HALO * j, 1) if j else before_all
            shift = (HALO * (strips - j)) % LANES
            after_all = pltpu.roll(after_all, shift, 1) if shift else after_all
            for r in range(0, group, chunk):
                at = j * group + r
                first, final = outer_strips(
                    inputs[comp][at:at + chunk, :LANES], inputs[comp][at:at + chunk, last:],
                    before_all[r:r + chunk], after_all[r:r + chunk], chunk)
                strip_a[comp * strips, top + at:top + at + chunk, :] = first
                strip_a[comp * strips + strips - 1, top + at:top + at + chunk, :] = final

    k_top = turns_ref[t]
    k_bottom = (4 - turns_ref[down]) & 3
    for side, turns, at in ((0, k_top, MARGIN), (1, k_bottom, top + rows)):
        pair = turn(in_rows[side, 0], in_rows[side, 1], turns)
        before = turn(in_corners[2 * side, 0], in_corners[2 * side, 1], turns)
        after = turn(in_corners[2 * side + 1, 0], in_corners[2 * side + 1, 1], turns)
        for comp in range(PAIR):
            x = [pair[comp][:, k * LANES:(k + 1) * LANES] for k in range(cols // LANES)]
            first, final = outer_strips(
                x[0], x[-1], pltpu.roll(before[comp], HALO, 1),
                pltpu.roll(after[comp], HALO * strips, 1), HALO)
            for s, value in enumerate([first] + split_strips(x, HALO) + [final]):
                strip_a[comp * strips + s, at:at + HALO, :] = value

    inner = rows + 2 * HALO

    def one_pass(src, dst, job):
        for r in range(MARGIN, MARGIN + inner, chunk):
            mid = src[job, r:r + chunk, :]
            around = src[job, r - 1:r - 1 + chunk, :] + src[job, r + 1:r + 1 + chunk, :]
            beside = pltpu.roll(mid, 1, 1) + pltpu.roll(mid, LANES - 1, 1)
            dst[job, r:r + chunk, :] = (mid + around) + beside

    def two_passes(_, job):
        one_pass(strip_a, strip_b, job)
        one_pass(strip_b, strip_a, job)
        return job

    def filter_strip(job, carry):
        lax.fori_loop(0, PASSES // 2, two_passes, job)
        return carry

    lax.fori_loop(0, PAIR * strips, filter_strip, 0)

    side_rows = rows // 4
    for comp in range(PAIR):
        for s in range(strips):
            job = comp * strips + s
            where = slice(s * LANES, (s + 1) * LANES)
            row_sums[comp, 8:8 + side_rows, where] = (
                (strip_a[job, pl.ds(top, side_rows, stride=4), :]
                 + strip_a[job, pl.ds(top + 1, side_rows, stride=4), :])
                + (strip_a[job, pl.ds(top + 2, side_rows, stride=4), :]
                   + strip_a[job, pl.ds(top + 3, side_rows, stride=4), :]))
            row_sums[comp, 7:8, where] = jnp.sum(strip_a[job, top - 4:top, :], axis=0, keepdims=True)
            row_sums[comp, 8 + side_rows:9 + side_rows, where] = jnp.sum(
                strip_a[job, top + rows:top + rows + 4, :], axis=0, keepdims=True)

    scale = KAPPA ** PASSES / 16.0
    for comp in range(PAIR):
        x = row_sums[comp]
        high = x.astype(jnp.bfloat16)
        rest = x - high.astype(jnp.float32)
        mid = rest.astype(jnp.bfloat16)
        low = (rest - mid.astype(jnp.float32)).astype(jnp.bfloat16)
        w = weights[...]
        z = (jnp.dot(low, w, preferred_element_type=jnp.float32)
             + jnp.dot(mid, w, preferred_element_type=jnp.float32)
             + jnp.dot(high, w, preferred_element_type=jnp.float32))
        centre[comp] = z[:, :LANES] * scale
        across[comp] = z[:, LANES:] * (0.5 * scale)

    for r in range(0, side_rows, chunk):
        u_dx = across[0, 8 + r:8 + r + chunk, :]
        v_dx = across[1, 8 + r:8 + r + chunk, :]
        u_dy = (centre[0, 9 + r:9 + r + chunk, :] - centre[0, 7 + r:7 + r + chunk, :]) * 0.5
        v_dy = (centre[1, 9 + r:9 + r + chunk, :] - centre[1, 7 + r:7 + r + chunk, :]) * 0.5
        fields[0, r:r + chunk, :] = centre[0, 8 + r:8 + r + chunk, :]
        fields[1, r:r + chunk, :] = centre[1, 8 + r:8 + r + chunk, :]
        fields[2, r:r + chunk, :] = v_dx - u_dy
        fields[3, r:r + chunk, :] = u_dy + v_dx
        fields[4, r:r + chunk, :] = u_dx - v_dy

    ts = side_rows // grid_x
    per = LANES // ts
    lane = lanes_of((8, LANES)) // ts
    for a in range(grid_x):
        live = [jnp.where(mask_ref[a, e] == 1, 1.0, 0.0).astype(jnp.float32) for e in range(grid_y)]
        for f in range(5):
            parts = [fields[f, pl.ds(a * ts + j, 8, stride=per), :] for j in range(per)]
            for e in range(grid_y):
                value = parts[e]
                for j in range(per):
                    if j != e:
                        value = jnp.where(lane == j, pltpu.roll(parts[j], ((j - e) * ts) % LANES, 1), value)
                tiles[a * grid_y + e, f] = value * live[e]

    for q in range(count):
        out_tiles[q // slots, q % slots] = tiles[pick[q]] * kept[q]

    sends = []
    for d in range(1, n_tile):
        peer = lax.rem(t + d, n_tile)
        copy = pltpu.make_async_remote_copy(
            src_ref=out_tiles.at[peer], dst_ref=in_tiles.at[t],
            send_sem=all_send.at[d], recv_sem=all_recv.at[d],
            device_id=(peer, c), device_id_type=MESH)
        copy.start()
        sends.append(copy)
    own = pltpu.make_async_copy(out_tiles.at[t], in_tiles.at[t], own_sem)
    own.start()

    def term_step(h, carry):
        base = tiles[h]
        for n, value in enumerate(make_terms(*[base[f] for f in range(5)])):
            terms[n, h] = value
        return carry

    lax.fori_loop(0, count, term_step, 0)
    gram_lane = lanes_of((TERMS, LANES))

    def gram_step(n, carry):
        mine = terms[n]
        sums = [jnp.sum(jnp.sum(mine * terms[m], axis=0), axis=0, keepdims=True) for m in range(TERMS)]
        column = jnp.sum(jnp.concatenate(sums, axis=0), axis=1, keepdims=True)
        return jnp.where(gram_lane == n, column, carry)

    part = lax.fori_loop(0, TERMS, gram_step, jnp.zeros((TERMS, LANES), jnp.float32))
    gram_out[...] = part
    gram_in[t] = part
    first_sums = []
    for d in range(1, n_tile):
        copy = pltpu.make_async_remote_copy(
            src_ref=gram_out, dst_ref=gram_in.at[t],
            send_sem=sum_send.at[d], recv_sem=sum_recv.at[d],
            device_id=(lax.rem(t + d, n_tile), c), device_id_type=MESH)
        copy.start()
        first_sums.append(copy)
    for copy in first_sums:
        copy.wait()
    part = jnp.sum(gram_in[...], axis=0)
    gram_out2[...] = part
    gram_in2[c] = part
    second_sums = []
    for d in range(1, n_col):
        copy = pltpu.make_async_remote_copy(
            src_ref=gram_out2, dst_ref=gram_in2.at[c],
            send_sem=sum2_send.at[d], recv_sem=sum2_recv.at[d],
            device_id=(t, lax.rem(c + d, n_col)), device_id_type=MESH)
        copy.start()
        second_sums.append(copy)

    own.wait()
    for copy in sends:
        copy.wait()

    def library_step(q, carry):
        base = in_tiles[q // slots, q % slots]
        for n, value in enumerate(make_terms(*[base[f] for f in range(5)])):
            block_terms[n * 8:(n + 1) * 8, :] = value
        for s in range(8):
            library_ref[0, 0, q, :, s * LANES:(s + 1) * LANES] = block_terms[pl.ds(s, TERMS, stride=8), :]
        return carry

    lax.fori_loop(0, count, library_step, 0)

    for copy in second_sums:
        copy.wait()
    gram = jnp.sum(gram_in2[...], axis=0) / (side_rows * side_rows)
    gram_ref[...] = gram[:, :TERMS]


def per_device(n_tile, n_col, u_velocity, v_velocity, ocean_mask, tile_owner, lower_edge_quarter_turns):
    rows, cols = u_velocity.shape
    grid_x, grid_y = ocean_mask.shape
    count = grid_x * grid_y
    slots = count // n_tile
    strips = cols // LANES + 1
    height = rows + 2 * HALO + 2 * MARGIN
    side_rows = rows // 4
    cells = (side_rows // grid_x) ** 2
    vmem = pl.BlockSpec(memory_space=pltpu.VMEM)
    smem = pl.BlockSpec(memory_space=pltpu.SMEM)
    f32 = jnp.float32
    return pl.pallas_call(
        functools.partial(kernel, n_tile, n_col, grid_x, grid_y),
        out_shape=(
            jax.ShapeDtypeStruct((1, 1, count, TERMS, cells), f32),
            jax.ShapeDtypeStruct((TERMS, TERMS), f32),
        ),
        in_specs=[vmem, vmem, smem, smem, smem],
        out_specs=(vmem, vmem),
        scratch_shapes=[
            pltpu.VMEM((PAIR * strips, height, LANES), f32),
            pltpu.VMEM((PAIR * strips, height, LANES), f32),
            pltpu.VMEM((strips * LANES, 2 * LANES), jnp.bfloat16),
            pltpu.VMEM((PAIR, side_rows + 16, strips * LANES), f32),
            pltpu.VMEM((PAIR, side_rows + 16, LANES), f32),
            pltpu.VMEM((PAIR, side_rows + 16, LANES), f32),
            pltpu.VMEM((5, side_rows, LANES), f32),
            pltpu.VMEM((count, 5, 8, LANES), f32),
            pltpu.VMEM((TERMS, count, 8, LANES), f32),
            pltpu.VMEM((n_tile, slots, 5, 8, LANES), f32),
            pltpu.VMEM((n_tile, slots, 5, 8, LANES), f32),
            pltpu.VMEM((TERMS * 8, LANES), f32),
            pltpu.VMEM((2, PAIR, rows // 8, LANES), f32),
            pltpu.VMEM((2, PAIR, rows // 8, LANES), f32),
            pltpu.VMEM((2, PAIR, HALO, cols), f32),
            pltpu.VMEM((4, PAIR, HALO, LANES), f32),
            pltpu.VMEM((TERMS, LANES), f32),
            pltpu.VMEM((n_tile, TERMS, LANES), f32),
            pltpu.VMEM((TERMS, LANES), f32),
            pltpu.VMEM((n_col, TERMS, LANES), f32),
            pltpu.SMEM((count,), jnp.int32),
            pltpu.SMEM((count,), f32),
            pltpu.SemaphoreType.DMA((14,)),
            pltpu.SemaphoreType.DMA((14,)),
            pltpu.SemaphoreType.DMA((n_tile,)),
            pltpu.SemaphoreType.DMA((n_tile,)),
            pltpu.SemaphoreType.DMA((n_tile,)),
            pltpu.SemaphoreType.DMA((n_tile,)),
            pltpu.SemaphoreType.DMA((n_col,)),
            pltpu.SemaphoreType.DMA((n_col,)),
            pltpu.SemaphoreType.DMA,
        ],
        compiler_params=pltpu.CompilerParams(
            collective_id=0, has_side_effects=True, vmem_limit_bytes=40 * 1024 * 1024),
    )(u_velocity, v_velocity, ocean_mask, tile_owner, lower_edge_quarter_turns)


def solution(mesh):
    in_specs = (P("tile", "col"), P("tile", "col"), P("tile", "col"), P("tile", "col"), P())
    out_specs = (P("tile", "col", None, None, None), P())
    return jax.shard_map(
        functools.partial(per_device, mesh.shape["tile"], mesh.shape["col"]),
        mesh=mesh, in_specs=in_specs, out_specs=out_specs, check_vma=False,
    )
```

profile of v0, /device:TPU:0, one launch (start us, length us, event | category | flops | bytes accessed | tf_op | source)
XLA Modules:
  0.0 47.5 jit_solution(7268613437992798193)
XLA Ops:
  0.6 0.0 copy-start
  0.6 1.2 %copy-done = f32[512,512]{1,0:T(8,128)S(1)} copy-done((f32[512,512]{1,0:T(8,128)S(1)}, f32[512,512]{1,0:T(8,128)}, u32[]{:S(2)}) %copy-start) | copy-done | bytes 1048600
  1.9 0.0 copy-start.1
  1.9 1.2 %copy-done.1 = f32[512,512]{1,0:T(8,128)S(1)} copy-done((f32[512,512]{1,0:T(8,128)S(1)}, f32[512,512]{1,0:T(8,128)}, u32[]{:S(2)}) %copy-start.1) | copy-done | bytes 1048600
  3.1 0.0 copy-start.2
  3.1 0.7 %copy-done.2 = s32[4,4]{1,0:T(4,128)S(1)} copy-done((s32[4,4]{1,0:T(4,128)S(1)}, s32[4,4]{1,0:T(4,128)}, u32[]{:S(2)}) %copy-start.2) | copy-done | bytes 88
  3.8 0.0 copy-start.3
  3.8 0.7 %copy-done.3 = s32[4,4]{1,0:T(4,128)S(1)} copy-done((s32[4,4]{1,0:T(4,128)S(1)}, s32[4,4]{1,0:T(4,128)}, u32[]{:S(2)}) %copy-start.3) | copy-done | bytes 88
  4.4 0.0 copy-start.4
  4.4 0.7 %copy-done.4 = s32[8]{0:T(128)S(1)} copy-done((s32[8]{0:T(128)S(1)}, s32[8]{0:T(128)}, u32[]{:S(2)}) %copy-start.4) | copy-done | bytes 56
  5.1 40.8 %shard_map.68 = (f32[1,1,16,16,1024]{4,3,2,1,0:T(8,128)S(1)}, f32[16,16]{1,0:T(8,128)S(1)}) custom-call(f32[512,512]{1,0:T(8,128)S(1)} %copy-done, f32[512,512]{1,0:T(8,128)S(1)} %copy-done.1, s32[4,4]{1,0:T(4,128)S(1)} %copy-done.2, s32[4,4]{1,0:T(4,128)S(1)} %copy-done.3, s32[8]{0:T(128)S(1)} %copy-done.4), custom_call_target="tpu_custom_call" | custom-call | tf_op jit(solution)/shard_map/pallas_call | solution.py:348
  46.0 1.0 %copy.9 = f32[1,1,16,16,1024]{4,3,2,1,0:T(8,128)} copy(f32[1,1,16,16,1024]{4,3,2,1,0:T(8,128)S(1)} %get-tuple-element.4) | data formatting | bytes 2097152
  46.9 0.6 %copy.10 = f32[16,16]{1,0:T(8,128)} copy(f32[16,16]{1,0:T(8,128)S(1)} %get-tuple-element.5) | data formatting | bytes 2048
Async XLA Ops:
  0.6 1.2 %copy-start = (f32[512,512]{1,0:T(8,128)S(1)}, f32[512,512]{1,0:T(8,128)}, u32[]{:S(2)}) copy-start(f32[512,512]{1,0:T(8,128)} %u_ref.1) | copy-start | bytes 3145732
  1.9 1.2 %copy-start.1 = (f32[512,512]{1,0:T(8,128)S(1)}, f32[512,512]{1,0:T(8,128)}, u32[]{:S(2)}) copy-start(f32[512,512]{1,0:T(8,128)} %v_ref.1) | copy-start | bytes 3145732
  3.1 0.7 %copy-start.2 = (s32[4,4]{1,0:T(4,128)S(1)}, s32[4,4]{1,0:T(4,128)}, u32[]{:S(2)}) copy-start(s32[4,4]{1,0:T(4,128)} %mask_ref.1) | copy-start | bytes 196
  3.8 0.7 %copy-start.3 = (s32[4,4]{1,0:T(4,128)S(1)}, s32[4,4]{1,0:T(4,128)}, u32[]{:S(2)}) copy-start(s32[4,4]{1,0:T(4,128)} %owner_ref.1) | copy-start | bytes 196
  4.4 0.7 %copy-start.4 = (s32[8]{0:T(128)S(1)}, s32[8]{0:T(128)}, u32[]{:S(2)}) copy-start(s32[8]{0:T(128)} %turns_ref.1) | copy-start | bytes 100
where the time goes:
time: 47.8 us; the launch traced here: 47.5 us
  Pallas kernels  40.8 us (85%)
  local copies, waits for them, and re-layouts  6.03 us (13%)
  between operations  0.65 us (1%)
    pallas_call x1, Pallas kernels, per_device(): pl.pallas_call(functools.partial(kernel, n_tile, n_col, grid_x, grid_y),...  40.8 us
    unnamed x12, local copies, waits for them, and re-layouts  6.03 us

commit v1 on v0

--- a/solution.py
+++ b/solution.py
@@ -12,7 +12,6 @@
 TERMS = 16
 LANES = 128
 HALO = 16
-MARGIN = 8
 STEP = 112
 PAIR = 2
 MESH = pl.DeviceIdType.MESH
@@ -36,21 +35,23 @@
     ]
 
 
-def kernel(n_tile, n_col, grid_x, grid_y, u_ref, v_ref, mask_ref, owner_ref, turns_ref,
-           library_ref, gram_ref, strip_a, strip_b, weights, row_sums, centre, across, fields,
-           tiles, terms, out_tiles, in_tiles, block_terms, pack, in_cols, in_rows, in_corners,
-           gram_out, gram_in, gram_out2, gram_in2, pick, kept,
+def kernel(n_tile, n_col, grid_x, grid_y, u_hbm, v_hbm, mask_hbm, owner_hbm, turns_hbm,
+           library_hbm, gram_ref, library_ref, inputs, mask_ref, owner_ref, turns_ref, strip_a, strip_b, strip_c,
+           weights, row_sums, centre, across, fields,
+           tiles, terms, products, out_tiles, in_tiles, block_terms, pack, in_cols, in_rows, in_corners,
+           gram_out, gram_in, gram_out2, gram_in2, pick, kept, load_sem,
            halo_send, halo_recv, all_send, all_recv, sum_send, sum_recv, sum2_send, sum2_recv,
-           own_sem):
+           own_sem, store_sem):
     t = lax.axis_index("tile")
     c = lax.axis_index("col")
     up, down = lax.rem(t + n_tile - 1, n_tile), lax.rem(t + 1, n_tile)
     left, right = lax.rem(c + n_col - 1, n_col), lax.rem(c + 1, n_col)
-    rows, cols = u_ref.shape
+    rows, cols = u_hbm.shape
     count = grid_x * grid_y
     slots = count // n_tile
-    inputs = (u_ref, v_ref)
+    sources = (u_hbm, v_hbm)
     last = cols - LANES
+    blocks = cols // LANES
 
     tile_peers = [(lax.rem(t + d, n_tile), c) for d in range(1, n_tile)]
     col_peers = [(t, lax.rem(c + d, n_col)) for d in range(1, n_col)]
@@ -60,6 +61,22 @@
     for peer in everyone:
         pl.semaphore_signal(barrier, inc=1, device_id=peer, device_id_type=MESH)
 
+    loads = []
+
+    def load(src, dst):
+        copy = pltpu.make_async_copy(src, dst, load_sem.at[len(loads)])
+        copy.start()
+        loads.append(copy)
+
+    for k in [0, blocks - 1] + list(range(1, blocks - 1)):
+        for comp in range(PAIR):
+            load(sources[comp].at[:, pl.ds(k * LANES, LANES)], inputs.at[comp, k])
+    load(mask_hbm, mask_ref)
+    load(owner_hbm, owner_ref)
+    load(turns_hbm, turns_ref)
+    for copy in loads[:2 * PAIR]:
+        copy.wait()
+
     group = rows // 8
     lane = lanes_of((group, LANES))
     for comp in range(PAIR):
@@ -67,9 +84,9 @@
         final = jnp.zeros((group, LANES), jnp.float32)
         for j in range(8):
             here = (lane >= HALO * j) & (lane < HALO * (j + 1))
-            block = inputs[comp][j * group:(j + 1) * group, :LANES]
+            block = inputs[comp, 0, j * group:(j + 1) * group, :]
             first = jnp.where(here, pltpu.roll(block, HALO * j, 1) if j else block, first)
-            block = inputs[comp][j * group:(j + 1) * group, last:]
+            block = inputs[comp, blocks - 1, j * group:(j + 1) * group, :]
             final = jnp.where(here, pltpu.roll(block, HALO * (j + 1), 1) if j < 7 else block, final)
         pack[0, comp] = first
         pack[1, comp] = final
@@ -89,15 +106,18 @@
     send(pack.at[1], in_cols.at[0], (t, right))
     send(pack.at[0], in_cols.at[1], (t, left))
     for comp in range(PAIR):
-        send(inputs[comp].at[pl.ds(rows - HALO, HALO), :], in_rows.at[0, comp], (down, c))
-        send(inputs[comp].at[pl.ds(0, HALO), :], in_rows.at[1, comp], (up, c))
-    for comp in range(PAIR):
-        low = inputs[comp].at[pl.ds(rows - HALO, HALO), :]
-        high = inputs[comp].at[pl.ds(0, HALO), :]
+        send(sources[comp].at[pl.ds(rows - HALO, HALO), :], in_rows.at[0, comp], (down, c))
+        send(sources[comp].at[pl.ds(0, HALO), :], in_rows.at[1, comp], (up, c))
+    for comp in range(PAIR):
+        low = sources[comp].at[pl.ds(rows - HALO, HALO), :]
+        high = sources[comp].at[pl.ds(0, HALO), :]
         send(low.at[:, pl.ds(last, LANES)], in_corners.at[0, comp], (down, right))
         send(low.at[:, pl.ds(0, LANES)], in_corners.at[1, comp], (down, left))
         send(high.at[:, pl.ds(last, LANES)], in_corners.at[2, comp], (up, right))
         send(high.at[:, pl.ds(0, LANES)], in_corners.at[3, comp], (up, left))
+
+    for copy in loads[2 * PAIR:]:
+        copy.wait()
 
     for o in range(n_tile):
         seen = jnp.int32(0)
@@ -123,15 +143,6 @@
         minus = (jnp.logical_not(low_half)) & (target - 1 == from_col)
         value = jnp.where(plus, 1.0, jnp.where(minus, -1.0, 0.0))
         weights[s * LANES:(s + 1) * LANES, :] = jnp.where(valid, value, 0.0).astype(jnp.bfloat16)
-    row_sums[...] = jnp.zeros(row_sums.shape, jnp.float32)
-    for job in range(PAIR * strips):
-        edge = jnp.zeros((MARGIN, LANES), jnp.float32)
-        total = strip_a.shape[1]
-        strip_a[job, 0:MARGIN, :] = edge
-        strip_a[job, total - MARGIN:total, :] = edge
-        strip_b[job, 0:MARGIN, :] = edge
-        strip_b[job, total - MARGIN:total, :] = edge
-
     def split_strips(x, height):
         lane = lanes_of((height, LANES))
         out = []
@@ -145,11 +156,11 @@
         return (jnp.where(lane < HALO, before, pltpu.roll(x0, HALO, 1)),
                 jnp.where(lane < HALO * strips, pltpu.roll(x3, HALO * strips, 1), after))
 
-    top = MARGIN + HALO
+    top = HALO
     chunk = 32
     for comp in range(PAIR):
         for r in range(0, rows, chunk):
-            x = [inputs[comp][r:r + chunk, k * LANES:(k + 1) * LANES] for k in range(cols // LANES)]
+            x = [inputs[comp, k, r:r + chunk, :] for k in range(blocks)]
             for s, value in enumerate(split_strips(x, chunk)):
                 strip_a[comp * strips + s + 1, top + r:top + r + chunk, :] = value
 
@@ -166,14 +177,14 @@
             for r in range(0, group, chunk):
                 at = j * group + r
                 first, final = outer_strips(
-                    inputs[comp][at:at + chunk, :LANES], inputs[comp][at:at + chunk, last:],
+                    inputs[comp, 0, at:at + chunk, :], inputs[comp, blocks - 1, at:at + chunk, :],
                     before_all[r:r + chunk], after_all[r:r + chunk], chunk)
                 strip_a[comp * strips, top + at:top + at + chunk, :] = first
                 strip_a[comp * strips + strips - 1, top + at:top + at + chunk, :] = final
 
     k_top = turns_ref[t]
     k_bottom = (4 - turns_ref[down]) & 3
-    for side, turns, at in ((0, k_top, MARGIN), (1, k_bottom, top + rows)):
+    for side, turns, at in ((0, k_top, 0), (1, k_bottom, top + rows)):
         pair = turn(in_rows[side, 0], in_rows[side, 1], turns)
         before = turn(in_corners[2 * side, 0], in_corners[2 * side, 1], turns)
         after = turn(in_corners[2 * side + 1, 0], in_corners[2 * side + 1, 1], turns)
@@ -185,43 +196,55 @@
             for s, value in enumerate([first] + split_strips(x, HALO) + [final]):
                 strip_a[comp * strips + s, at:at + HALO, :] = value
 
-    inner = rows + 2 * HALO
-
-    def one_pass(src, dst, job):
-        for r in range(MARGIN, MARGIN + inner, chunk):
-            mid = src[job, r:r + chunk, :]
-            around = src[job, r - 1:r - 1 + chunk, :] + src[job, r + 1:r + 1 + chunk, :]
-            beside = pltpu.roll(mid, 1, 1) + pltpu.roll(mid, LANES - 1, 1)
-            dst[job, r:r + chunk, :] = (mid + around) + beside
-
-    def two_passes(_, job):
-        one_pass(strip_a, strip_b, job)
-        one_pass(strip_b, strip_a, job)
-        return job
+    depth = (rows + 2 * HALO) // 8
+
+    def five(above, mid, below):
+        return (mid + (above + below)) + (pltpu.roll(mid, 1, 1) + pltpu.roll(mid, LANES - 1, 1))
+
+    def two_passes(fetch, emit):
+        def get(k):
+            if k < 0:
+                return pltpu.roll(fetch(k + depth), 1, 0)
+            if k >= depth:
+                return pltpu.roll(fetch(k - depth), 7, 0)
+            return fetch(k)
+
+        x0, x1 = get(-2), get(-1)
+        y0 = y1 = None
+        for k in range(-1, depth + 1):
+            x2 = get(k + 1)
+            y2 = five(x0, x1, x2)
+            if k >= 1:
+                emit(k - 1, five(y0, y1, y2))
+            x0, x1, y0, y1 = x1, x2, y1, y2
 
     def filter_strip(job, carry):
-        lax.fori_loop(0, PASSES // 2, two_passes, job)
+        def put(dst):
+            def emit(k, value):
+                dst[k * 8:(k + 1) * 8, :] = value
+            return emit
+
+        quad = []
+
+        def emit_sums(k, value):
+            quad.append(value)
+            if len(quad) == 4:
+                row_sums[job, pl.ds(k // 4, 8, stride=depth // 4), :] = (quad[0] + quad[1]) + (quad[2] + quad[3])
+                quad.clear()
+
+        two_passes(lambda k: strip_a[job, pl.ds(k, 8, stride=depth), :], put(strip_b))
+        two_passes(lambda k: strip_b[k * 8:(k + 1) * 8, :], put(strip_c))
+        two_passes(lambda k: strip_c[k * 8:(k + 1) * 8, :], put(strip_b))
+        two_passes(lambda k: strip_b[k * 8:(k + 1) * 8, :], emit_sums)
         return carry
 
     lax.fori_loop(0, PAIR * strips, filter_strip, 0)
 
     side_rows = rows // 4
-    for comp in range(PAIR):
-        for s in range(strips):
-            job = comp * strips + s
-            where = slice(s * LANES, (s + 1) * LANES)
-            row_sums[comp, 8:8 + side_rows, where] = (
-                (strip_a[job, pl.ds(top, side_rows, stride=4), :]
-                 + strip_a[job, pl.ds(top + 1, side_rows, stride=4), :])
-                + (strip_a[job, pl.ds(top + 2, side_rows, stride=4), :]
-                   + strip_a[job, pl.ds(top + 3, side_rows, stride=4), :]))
-            row_sums[comp, 7:8, where] = jnp.sum(strip_a[job, top - 4:top, :], axis=0, keepdims=True)
-            row_sums[comp, 8 + side_rows:9 + side_rows, where] = jnp.sum(
-                strip_a[job, top + rows:top + rows + 4, :], axis=0, keepdims=True)
-
+    edge = HALO // 4
     scale = KAPPA ** PASSES / 16.0
     for comp in range(PAIR):
-        x = row_sums[comp]
+        x = jnp.concatenate([row_sums[comp * strips + s] for s in range(strips)], axis=1)
         high = x.astype(jnp.bfloat16)
         rest = x - high.astype(jnp.float32)
         mid = rest.astype(jnp.bfloat16)
@@ -234,12 +257,12 @@
         across[comp] = z[:, LANES:] * (0.5 * scale)
 
     for r in range(0, side_rows, chunk):
-        u_dx = across[0, 8 + r:8 + r + chunk, :]
-        v_dx = across[1, 8 + r:8 + r + chunk, :]
-        u_dy = (centre[0, 9 + r:9 + r + chunk, :] - centre[0, 7 + r:7 + r + chunk, :]) * 0.5
-        v_dy = (centre[1, 9 + r:9 + r + chunk, :] - centre[1, 7 + r:7 + r + chunk, :]) * 0.5
-        fields[0, r:r + chunk, :] = centre[0, 8 + r:8 + r + chunk, :]
-        fields[1, r:r + chunk, :] = centre[1, 8 + r:8 + r + chunk, :]
+        u_dx = across[0, edge + r:edge + r + chunk, :]
+        v_dx = across[1, edge + r:edge + r + chunk, :]
+        u_dy = (centre[0, edge + 1 + r:edge + 1 + r + chunk, :] - centre[0, edge - 1 + r:edge - 1 + r + chunk, :]) * 0.5
+        v_dy = (centre[1, edge + 1 + r:edge + 1 + r + chunk, :] - centre[1, edge - 1 + r:edge - 1 + r + chunk, :]) * 0.5
+        fields[0, r:r + chunk, :] = centre[0, edge + r:edge + r + chunk, :]
+        fields[1, r:r + chunk, :] = centre[1, edge + r:edge + r + chunk, :]
         fields[2, r:r + chunk, :] = v_dx - u_dy
         fields[3, r:r + chunk, :] = u_dy + v_dx
         fields[4, r:r + chunk, :] = u_dx - v_dy
@@ -280,15 +303,21 @@
         return carry
 
     lax.fori_loop(0, count, term_step, 0)
-    gram_lane = lanes_of((TERMS, LANES))
 
     def gram_step(n, carry):
         mine = terms[n]
-        sums = [jnp.sum(jnp.sum(mine * terms[m], axis=0), axis=0, keepdims=True) for m in range(TERMS)]
-        column = jnp.sum(jnp.concatenate(sums, axis=0), axis=1, keepdims=True)
-        return jnp.where(gram_lane == n, column, carry)
-
-    part = lax.fori_loop(0, TERMS, gram_step, jnp.zeros((TERMS, LANES), jnp.float32))
+        for m in range(TERMS):
+            products[n, m * 8:(m + 1) * 8, :] = jnp.sum(mine * terms[m], axis=0)
+        return carry
+
+    lax.fori_loop(0, TERMS, gram_step, 0)
+    gram_lane = lanes_of((TERMS, LANES))
+    part = jnp.zeros((TERMS, LANES), jnp.float32)
+    for n in range(TERMS):
+        sums = products[n, pl.ds(0, TERMS, stride=8), :]
+        for q in range(1, 8):
+            sums = sums + products[n, pl.ds(q, TERMS, stride=8), :]
+        part = jnp.where(gram_lane == n, jnp.sum(sums, axis=1, keepdims=True), part)
     gram_out[...] = part
     gram_in[t] = part
     first_sums = []
@@ -299,6 +328,27 @@
             device_id=(lax.rem(t + d, n_tile), c), device_id_type=MESH)
         copy.start()
         first_sums.append(copy)
+
+    def library_step(q, carry):
+        base = in_tiles[q // slots, q % slots]
+        for n, value in enumerate(make_terms(*[base[f] for f in range(5)])):
+            block_terms[n * 8:(n + 1) * 8, :] = value
+        for s in range(8):
+            library_ref[q, :, s * LANES:(s + 1) * LANES] = block_terms[pl.ds(s, TERMS, stride=8), :]
+        return carry
+
+    own.wait()
+    for copy in sends:
+        copy.wait()
+    half = count // 2
+    stores = [
+        pltpu.make_async_copy(library_ref.at[pl.ds(k * half, half)],
+                              library_hbm.at[0, 0, pl.ds(k * half, half)], store_sem.at[k])
+        for k in range(2)
+    ]
+    lax.fori_loop(0, half, library_step, 0)
+    stores[0].start()
+
     for copy in first_sums:
         copy.wait()
     part = jnp.sum(gram_in[...], axis=0)
@@ -313,24 +363,14 @@
         copy.start()
         second_sums.append(copy)
 
-    own.wait()
-    for copy in sends:
-        copy.wait()
-
-    def library_step(q, carry):
-        base = in_tiles[q // slots, q % slots]
-        for n, value in enumerate(make_terms(*[base[f] for f in range(5)])):
-            block_terms[n * 8:(n + 1) * 8, :] = value
-        for s in range(8):
-            library_ref[0, 0, q, :, s * LANES:(s + 1) * LANES] = block_terms[pl.ds(s, TERMS, stride=8), :]
-        return carry
-
-    lax.fori_loop(0, count, library_step, 0)
-
+    lax.fori_loop(half, count, library_step, 0)
+    stores[1].start()
     for copy in second_sums:
         copy.wait()
     gram = jnp.sum(gram_in2[...], axis=0) / (side_rows * side_rows)
     gram_ref[...] = gram[:, :TERMS]
+    for copy in stores:
+        copy.wait()
 
 
 def per_device(n_tile, n_col, u_velocity, v_velocity, ocean_mask, tile_owner, lower_edge_quarter_turns):
@@ -339,11 +379,11 @@
     count = grid_x * grid_y
     slots = count // n_tile
     strips = cols // LANES + 1
-    height = rows + 2 * HALO + 2 * MARGIN
+    height = rows + 2 * HALO
     side_rows = rows // 4
     cells = (side_rows // grid_x) ** 2
     vmem = pl.BlockSpec(memory_space=pltpu.VMEM)
-    smem = pl.BlockSpec(memory_space=pltpu.SMEM)
+    hbm = pl.BlockSpec(memory_space=pltpu.HBM)
     f32 = jnp.float32
     return pl.pallas_call(
         functools.partial(kernel, n_tile, n_col, grid_x, grid_y),
@@ -351,18 +391,25 @@
             jax.ShapeDtypeStruct((1, 1, count, TERMS, cells), f32),
             jax.ShapeDtypeStruct((TERMS, TERMS), f32),
         ),
-        in_specs=[vmem, vmem, smem, smem, smem],
-        out_specs=(vmem, vmem),
+        in_specs=[hbm] * 5,
+        out_specs=(hbm, vmem),
         scratch_shapes=[
+            pltpu.VMEM((count, TERMS, cells), f32),
+            pltpu.VMEM((PAIR, cols // LANES, rows, LANES), f32),
+            pltpu.SMEM(ocean_mask.shape, jnp.int32),
+            pltpu.SMEM(tile_owner.shape, jnp.int32),
+            pltpu.SMEM(lower_edge_quarter_turns.shape, jnp.int32),
             pltpu.VMEM((PAIR * strips, height, LANES), f32),
-            pltpu.VMEM((PAIR * strips, height, LANES), f32),
+            pltpu.VMEM((height, LANES), f32),
+            pltpu.VMEM((height, LANES), f32),
             pltpu.VMEM((strips * LANES, 2 * LANES), jnp.bfloat16),
-            pltpu.VMEM((PAIR, side_rows + 16, strips * LANES), f32),
-            pltpu.VMEM((PAIR, side_rows + 16, LANES), f32),
-            pltpu.VMEM((PAIR, side_rows + 16, LANES), f32),
+            pltpu.VMEM((PAIR * strips, height // 4, LANES), f32),
+            pltpu.VMEM((PAIR, height // 4, LANES), f32),
+            pltpu.VMEM((PAIR, height // 4, LANES), f32),
             pltpu.VMEM((5, side_rows, LANES), f32),
             pltpu.VMEM((count, 5, 8, LANES), f32),
             pltpu.VMEM((TERMS, count, 8, LANES), f32),
+            pltpu.VMEM((TERMS, TERMS * 8, LANES), f32),
             pltpu.VMEM((n_tile, slots, 5, 8, LANES), f32),
             pltpu.VMEM((n_tile, slots, 5, 8, LANES), f32),
             pltpu.VMEM((TERMS * 8, LANES), f32),
@@ -376,6 +423,7 @@
             pltpu.VMEM((n_col, TERMS, LANES), f32),
             pltpu.SMEM((count,), jnp.int32),
             pltpu.SMEM((count,), f32),
+            pltpu.SemaphoreType.DMA((PAIR * (cols // LANES) + 3,)),
             pltpu.SemaphoreType.DMA((14,)),
             pltpu.SemaphoreType.DMA((14,)),
             pltpu.SemaphoreType.DMA((n_tile,)),
@@ -385,9 +433,10 @@
             pltpu.SemaphoreType.DMA((n_col,)),
             pltpu.SemaphoreType.DMA((n_col,)),
             pltpu.SemaphoreType.DMA,
+            pltpu.SemaphoreType.DMA((2,)),
         ],
         compiler_params=pltpu.CompilerParams(
-            collective_id=0, has_side_effects=True, vmem_limit_bytes=40 * 1024 * 1024),
+            collective_id=0, has_side_effects=True, vmem_limit_bytes=60 * 1024 * 1024),
     )(u_velocity, v_velocity, ocean_mask, tile_owner, lower_edge_quarter_turns)
 
 

time: 47.8 us -> 120 us (2.51)
  Pallas kernels: 40.8 us -> 116 us
  local copies, waits for them, and re-layouts: 6.03 us -> 2.91 us
    pallas_call x1, Pallas kernels: 40.8 us -> 116 us  [per_device(): pl.pallas_call(functools.partial(kernel, n_tile, n_col, grid_x, grid_y),...]
    unnamed x12 -> x4, local copies, waits for them, and re-layouts: 6.03 us -> 2.91 us
where the time goes in v1:
time: 120 us
  Pallas kernels  116 us (97%)
  local copies, waits for them, and re-layouts  2.91 us (2%)
    pallas_call x1, Pallas kernels, per_device(): pl.pallas_call(functools.partial(kernel, n_tile, n_col, grid_x, grid_y),...  116 us
    unnamed x4, local copies, waits for them, and re-layouts  2.91 us

profile of v1, /device:TPU:0, one launch (start us, length us, event | category | flops | bytes accessed | tf_op | source)
XLA Modules:
  0.0 119.8 jit_solution(7358912013431124186)
XLA Ops:
  0.6 116.3 %shard_map.68 = (f32[1,1,16,16,1024]{4,3,2,1,0:T(8,128)}, f32[16,16]{1,0:T(8,128)}) custom-call(f32[512,512]{1,0:T(8,128)} %u_hbm.1, f32[512,512]{1,0:T(8,128)} %v_hbm.1, s32[4,4]{1,0:T(4,128)} %mask_hbm.1, s32[4,4]{1,0:T(4,128)} %owner_hbm.1, s32[8]{0:T(128)} %turns_hbm.1), custom_call_target="tpu_custom_call" | custom-call | tf_op jit(solution)/shard_map/pallas_call | solution.py:388
  116.9 0.0 copy-start
  116.9 2.3 %copy.9 = f32[1,1,16,16,1024]{4,3,2,1,0:T(8,128)} copy(f32[1,1,16,16,1024]{4,3,2,1,0:T(8,128)} %get-tuple-element.4) | data formatting | bytes 2097152
  119.2 0.0 copy-done
  119.2 0.6 copy.10
Async XLA Ops:
  116.9 2.3 %copy-start = (f32[16,16]{1,0:T(8,128)S(1)}, f32[16,16]{1,0:T(8,128)}, u32[]{:S(2)}) copy-start(f32[16,16]{1,0:T(8,128)} %get-tuple-element.5) | copy-start | bytes 3076

commit v2 on v1

--- a/solution.py
+++ b/solution.py
@@ -198,44 +198,35 @@
 
     depth = (rows + 2 * HALO) // 8
 
-    def five(above, mid, below):
-        return (mid + (above + below)) + (pltpu.roll(mid, 1, 1) + pltpu.roll(mid, LANES - 1, 1))
-
-    def two_passes(fetch, emit):
-        def get(k):
-            if k < 0:
-                return pltpu.roll(fetch(k + depth), 1, 0)
-            if k >= depth:
-                return pltpu.roll(fetch(k - depth), 7, 0)
-            return fetch(k)
-
-        x0, x1 = get(-2), get(-1)
-        y0 = y1 = None
-        for k in range(-1, depth + 1):
-            x2 = get(k + 1)
-            y2 = five(x0, x1, x2)
-            if k >= 1:
-                emit(k - 1, five(y0, y1, y2))
-            x0, x1, y0, y1 = x1, x2, y1, y2
+    step = 8 * 10
+    inner = 8 * depth
+
+    def wrap(dst):
+        dst[0:8, :] = pltpu.roll(dst[inner:inner + 8, :], 1, 0)
+        dst[inner + 8:inner + 16, :] = pltpu.roll(dst[8:16, :], 7, 0)
+
+    def one_pass(src, dst):
+        for r in range(8, 8 + inner, step):
+            size = min(step, 8 + inner - r)
+            mid = src[r:r + size, :]
+            around = src[r - 8:r - 8 + size, :] + src[r + 8:r + 8 + size, :]
+            beside = pltpu.roll(mid, 1, 1) + pltpu.roll(mid, LANES - 1, 1)
+            dst[r:r + size, :] = (mid + around) + beside
+        wrap(dst)
+
+    def pass_pair(_, carry):
+        one_pass(strip_b, strip_c)
+        one_pass(strip_c, strip_b)
+        return carry
 
     def filter_strip(job, carry):
-        def put(dst):
-            def emit(k, value):
-                dst[k * 8:(k + 1) * 8, :] = value
-            return emit
-
-        quad = []
-
-        def emit_sums(k, value):
-            quad.append(value)
-            if len(quad) == 4:
-                row_sums[job, pl.ds(k // 4, 8, stride=depth // 4), :] = (quad[0] + quad[1]) + (quad[2] + quad[3])
-                quad.clear()
-
-        two_passes(lambda k: strip_a[job, pl.ds(k, 8, stride=depth), :], put(strip_b))
-        two_passes(lambda k: strip_b[k * 8:(k + 1) * 8, :], put(strip_c))
-        two_passes(lambda k: strip_c[k * 8:(k + 1) * 8, :], put(strip_b))
-        two_passes(lambda k: strip_b[k * 8:(k + 1) * 8, :], emit_sums)
+        for k in range(depth):
+            strip_b[(k + 1) * 8:(k + 2) * 8, :] = strip_a[job, pl.ds(k, 8, stride=depth), :]
+        wrap(strip_b)
+        lax.fori_loop(0, PASSES // 2, pass_pair, 0)
+        for k in range(0, depth, 4):
+            quad = [strip_b[(k + 1 + q) * 8:(k + 2 + q) * 8, :] for q in range(4)]
+            row_sums[job, pl.ds(k // 4, 8, stride=depth // 4), :] = (quad[0] + quad[1]) + (quad[2] + quad[3])
         return carry
 
     lax.fori_loop(0, PAIR * strips, filter_strip, 0)
@@ -400,8 +391,8 @@
             pltpu.SMEM(tile_owner.shape, jnp.int32),
             pltpu.SMEM(lower_edge_quarter_turns.shape, jnp.int32),
             pltpu.VMEM((PAIR * strips, height, LANES), f32),
-            pltpu.VMEM((height, LANES), f32),
-            pltpu.VMEM((height, LANES), f32),
+            pltpu.VMEM((height + 16, LANES), f32),
+            pltpu.VMEM((height + 16, LANES), f32),
             pltpu.VMEM((strips * LANES, 2 * LANES), jnp.bfloat16),
             pltpu.VMEM((PAIR * strips, height // 4, LANES), f32),
             pltpu.VMEM((PAIR, height // 4, LANES), f32),

time: 120 us -> 44.9 us (0.37)
  Pallas kernels: 116 us -> 41.1 us
    pallas_call x1, Pallas kernels: 116 us -> 41.1 us  [per_device(): pl.pallas_call(functools.partial(kernel, n_tile, n_col, grid_x, grid_y),...]
where the time goes in v2:
time: 44.9 us; the launch traced here: 44.7 us
  Pallas kernels  41.1 us (92%)
  local copies, waits for them, and re-layouts  2.91 us (6%)
  between operations  0.65 us (1%)
    pallas_call x1, Pallas kernels, per_device(): pl.pallas_call(functools.partial(kernel, n_tile, n_col, grid_x, grid_y),...  41.1 us
    unnamed x4, local copies, waits for them, and re-layouts  2.91 us

profile of v2, /device:TPU:0, one launch (start us, length us, event | category | flops | bytes accessed | tf_op | source)
XLA Modules:
  0.0 44.7 jit_solution(11807785880836819870)
XLA Ops:
  0.6 41.1 %shard_map.68 = (f32[1,1,16,16,1024]{4,3,2,1,0:T(8,128)}, f32[16,16]{1,0:T(8,128)}) custom-call(f32[512,512]{1,0:T(8,128)} %u_hbm.1, f32[512,512]{1,0:T(8,128)} %v_hbm.1, s32[4,4]{1,0:T(4,128)} %mask_hbm.1, s32[4,4]{1,0:T(4,128)} %owner_hbm.1, s32[8]{0:T(128)} %turns_hbm.1), custom_call_target="tpu_custom_call" | custom-call | tf_op jit(solution)/shard_map/pallas_call | solution.py:379
  41.8 0.0 copy-start
  41.8 2.3 %copy.9 = f32[1,1,16,16,1024]{4,3,2,1,0:T(8,128)} copy(f32[1,1,16,16,1024]{4,3,2,1,0:T(8,128)} %get-tuple-element.4) | data formatting | bytes 2097152
  44.1 0.0 copy-done
  44.1 0.6 %copy.10 = f32[16,16]{1,0:T(8,128)} copy(f32[16,16]{1,0:T(8,128)S(1)} %copy-done) | data formatting | bytes 2048
Async XLA Ops:
  41.8 2.3 %copy-start = (f32[16,16]{1,0:T(8,128)S(1)}, f32[16,16]{1,0:T(8,128)}, u32[]{:S(2)}) copy-start(f32[16,16]{1,0:T(8,128)} %get-tuple-element.5) | copy-start | bytes 3076

commit v3 on v2

--- a/solution.py
+++ b/solution.py
@@ -12,7 +12,6 @@
 TERMS = 16
 LANES = 128
 HALO = 16
-STEP = 112
 PAIR = 2
 MESH = pl.DeviceIdType.MESH
 
@@ -36,8 +35,8 @@
 
 
 def kernel(n_tile, n_col, grid_x, grid_y, u_hbm, v_hbm, mask_hbm, owner_hbm, turns_hbm,
-           library_hbm, gram_ref, library_ref, inputs, mask_ref, owner_ref, turns_ref, strip_a, strip_b, strip_c,
-           weights, row_sums, centre, across, fields,
+           library_hbm, gram_ref, library_ref, inputs, mask_ref, owner_ref, turns_ref, mixed, field_b, field_c,
+           spread, weights, row_sums, centre, across, fields,
            tiles, terms, products, out_tiles, in_tiles, block_terms, pack, in_cols, in_rows, in_corners,
            gram_out, gram_in, gram_out2, gram_in2, pick, kept, load_sem,
            halo_send, halo_recv, all_send, all_recv, sum_send, sum_recv, sum2_send, sum2_recv,
@@ -131,56 +130,63 @@
             pick[o * slots + p] = chosen[p]
             kept[o * slots + p] = jnp.where(seen > p, 1.0, 0.0).astype(jnp.float32)
 
-    strips = strip_a.shape[0] // PAIR
-    for s in range(strips):
-        spot = lax.broadcasted_iota(jnp.int32, (LANES, 2 * LANES), 0)
-        cell = lax.broadcasted_iota(jnp.int32, (LANES, 2 * LANES), 1)
-        from_col = (spot + (s * STEP - HALO)) >> 2
-        valid = (spot >= PASSES) & (spot < LANES - PASSES)
-        low_half = cell < LANES
-        target = jnp.where(low_half, cell, cell - LANES)
-        plus = jnp.where(low_half, target, target + 1) == from_col
-        minus = (jnp.logical_not(low_half)) & (target - 1 == from_col)
-        value = jnp.where(plus, 1.0, jnp.where(minus, -1.0, 0.0))
-        weights[s * LANES:(s + 1) * LANES, :] = jnp.where(valid, value, 0.0).astype(jnp.bfloat16)
-    def split_strips(x, height):
-        lane = lanes_of((height, LANES))
-        out = []
-        for s in range(1, strips - 1):
-            shift = HALO * (s + 1)
-            out.append(jnp.where(lane < shift, pltpu.roll(x[s - 1], shift, 1), pltpu.roll(x[s], shift, 1)))
-        return out
-
-    def outer_strips(x0, x3, before, after, height):
-        lane = lanes_of((height, LANES))
-        return (jnp.where(lane < HALO, before, pltpu.roll(x0, HALO, 1)),
-                jnp.where(lane < HALO * strips, pltpu.roll(x3, HALO * strips, 1), after))
+    planes = blocks + 1
+    spot = lax.broadcasted_iota(jnp.int32, (LANES, LANES), 0)
+    cell = lax.broadcasted_iota(jnp.int32, (LANES, LANES), 1)
+    for m in range(planes):
+        column = cell * planes + m
+        where = slice(m * LANES, (m + 1) * LANES)
+        for k in range(blocks):
+            spread[k * LANES:(k + 1) * LANES, where] = jnp.where(
+                spot + (k * LANES + HALO) == column, 1.0, 0.0).astype(jnp.bfloat16)
+        source = jnp.where(spot < HALO, spot, jnp.where(spot < 2 * HALO, spot + cols, -1))
+        spread[cols:, where] = jnp.where(source == column, 1.0, 0.0).astype(jnp.bfloat16)
+        from_col = (spot * planes + (m - HALO)) >> 2
+        weights[where, :LANES] = jnp.where(from_col == cell, 1.0, 0.0).astype(jnp.bfloat16)
+        weights[where, LANES:] = jnp.where(
+            from_col == cell + 1, 1.0, jnp.where(from_col == cell - 1, -1.0, 0.0)).astype(jnp.bfloat16)
+
+    def exact_dot(x, w):
+        high = x.astype(jnp.bfloat16)
+        low = (x - high.astype(jnp.float32)).astype(jnp.bfloat16)
+        return (jnp.dot(low, w, preferred_element_type=jnp.float32)
+                + jnp.dot(high, w, preferred_element_type=jnp.float32))
 
     top = HALO
     chunk = 32
+    part_rows = 128
+
+    def spread_rows(i, carry):
+        comp, r = i // (rows // part_rows), (i % (rows // part_rows)) * part_rows
+        r = pl.multiple_of(r, part_rows)
+        x = jnp.concatenate([inputs[comp, k, pl.ds(r, part_rows), :] for k in range(blocks)], axis=1)
+        y = exact_dot(x, spread[:cols, :])
+        for m in range(planes):
+            mixed[comp * planes + m, pl.ds(top + r, part_rows), :] = y[:, m * LANES:(m + 1) * LANES]
+        return carry
+
+    lax.fori_loop(0, PAIR * (rows // part_rows), spread_rows, 0)
+
+    for copy in copies:
+        copy.wait()
+
+    def rim(before, after, height):
+        lane = lanes_of((height, LANES))
+        return jnp.where(lane < HALO, before, jnp.where(lane < 2 * HALO, after, 0.0))
+
     for comp in range(PAIR):
-        for r in range(0, rows, chunk):
-            x = [inputs[comp, k, r:r + chunk, :] for k in range(blocks)]
-            for s, value in enumerate(split_strips(x, chunk)):
-                strip_a[comp * strips + s + 1, top + r:top + r + chunk, :] = value
-
-    for copy in copies:
-        copy.wait()
-
-    for comp in range(PAIR):
+        rims = []
         for j in range(8):
-            before_all = in_cols[0, comp]
-            after_all = in_cols[1, comp]
-            before_all = pltpu.roll(before_all, LANES - HALO * j, 1) if j else before_all
-            shift = (HALO * (strips - j)) % LANES
-            after_all = pltpu.roll(after_all, shift, 1) if shift else after_all
-            for r in range(0, group, chunk):
-                at = j * group + r
-                first, final = outer_strips(
-                    inputs[comp, 0, at:at + chunk, :], inputs[comp, blocks - 1, at:at + chunk, :],
-                    before_all[r:r + chunk], after_all[r:r + chunk], chunk)
-                strip_a[comp * strips, top + at:top + at + chunk, :] = first
-                strip_a[comp * strips + strips - 1, top + at:top + at + chunk, :] = final
+            before, after = in_cols[0, comp], in_cols[1, comp]
+            before = pltpu.roll(before, LANES - HALO * j, 1) if j else before
+            shift = (HALO * (1 - j)) % LANES
+            after = pltpu.roll(after, shift, 1) if shift else after
+            rims.append(rim(before, after, group))
+        for j in range(0, 8, 2):
+            y = exact_dot(jnp.concatenate(rims[j:j + 2], axis=0), spread[cols:, :])
+            for m in range(planes):
+                at = slice(top + j * group, top + (j + 2) * group)
+                mixed[comp * planes + m, at, :] += y[:, m * LANES:(m + 1) * LANES]
 
     k_top = turns_ref[t]
     k_bottom = (4 - turns_ref[down]) & 3
@@ -189,53 +195,62 @@
         before = turn(in_corners[2 * side, 0], in_corners[2 * side, 1], turns)
         after = turn(in_corners[2 * side + 1, 0], in_corners[2 * side + 1, 1], turns)
         for comp in range(PAIR):
-            x = [pair[comp][:, k * LANES:(k + 1) * LANES] for k in range(cols // LANES)]
-            first, final = outer_strips(
-                x[0], x[-1], pltpu.roll(before[comp], HALO, 1),
-                pltpu.roll(after[comp], HALO * strips, 1), HALO)
-            for s, value in enumerate([first] + split_strips(x, HALO) + [final]):
-                strip_a[comp * strips + s, at:at + HALO, :] = value
+            ends = rim(pltpu.roll(before[comp], HALO, 1), pltpu.roll(after[comp], HALO, 1), HALO)
+            y = exact_dot(jnp.concatenate([pair[comp], ends], axis=1), spread[...])
+            for m in range(planes):
+                mixed[comp * planes + m, at:at + HALO, :] = y[:, m * LANES:(m + 1) * LANES]
 
     depth = (rows + 2 * HALO) // 8
 
-    step = 8 * 10
     inner = 8 * depth
+    batch = depth // 4
 
     def wrap(dst):
-        dst[0:8, :] = pltpu.roll(dst[inner:inner + 8, :], 1, 0)
-        dst[inner + 8:inner + 16, :] = pltpu.roll(dst[8:16, :], 7, 0)
+        for m in range(planes):
+            dst[m, 0:8, :] = pltpu.roll(dst[m, inner:inner + 8, :], 1, 0)
+            dst[m, inner + 8:inner + 16, :] = pltpu.roll(dst[m, 8:16, :], 7, 0)
 
     def one_pass(src, dst):
-        for r in range(8, 8 + inner, step):
-            size = min(step, 8 + inner - r)
-            mid = src[r:r + size, :]
-            around = src[r - 8:r - 8 + size, :] + src[r + 8:r + 8 + size, :]
-            beside = pltpu.roll(mid, 1, 1) + pltpu.roll(mid, LANES - 1, 1)
-            dst[r:r + size, :] = (mid + around) + beside
+        def line(k):
+            return [src[m, k * 8:(k + 1) * 8, :] for m in range(planes)]
+
+        for k0 in range(1, depth + 1, batch):
+            lefts = [pltpu.roll(src[planes - 1, k * 8:(k + 1) * 8, :], 1, 1) for k in range(k0, k0 + batch)]
+            rights = [pltpu.roll(src[0, k * 8:(k + 1) * 8, :], LANES - 1, 1) for k in range(k0, k0 + batch)]
+            above, mid = line(k0 - 1), line(k0)
+            for k in range(k0, k0 + batch):
+                below = line(k + 1)
+                beside = [lefts[k - k0]] + mid + [rights[k - k0]]
+                for m in range(planes):
+                    dst[m, k * 8:(k + 1) * 8, :] = (mid[m] + (above[m] + below[m])) + (beside[m] + beside[m + 2])
+                above, mid = mid, below
         wrap(dst)
 
     def pass_pair(_, carry):
-        one_pass(strip_b, strip_c)
-        one_pass(strip_c, strip_b)
-        return carry
-
-    def filter_strip(job, carry):
-        for k in range(depth):
-            strip_b[(k + 1) * 8:(k + 2) * 8, :] = strip_a[job, pl.ds(k, 8, stride=depth), :]
-        wrap(strip_b)
+        one_pass(field_b, field_c)
+        one_pass(field_c, field_b)
+        return carry
+
+    def filter_field(comp, carry):
+        for m in range(planes):
+            for k in range(depth):
+                field_b[m, (k + 1) * 8:(k + 2) * 8, :] = mixed[comp * planes + m, pl.ds(k, 8, stride=depth), :]
+        wrap(field_b)
         lax.fori_loop(0, PASSES // 2, pass_pair, 0)
-        for k in range(0, depth, 4):
-            quad = [strip_b[(k + 1 + q) * 8:(k + 2 + q) * 8, :] for q in range(4)]
-            row_sums[job, pl.ds(k // 4, 8, stride=depth // 4), :] = (quad[0] + quad[1]) + (quad[2] + quad[3])
-        return carry
-
-    lax.fori_loop(0, PAIR * strips, filter_strip, 0)
+        for m in range(planes):
+            for k in range(0, depth, 4):
+                quad = [field_b[m, (k + 1 + q) * 8:(k + 2 + q) * 8, :] for q in range(4)]
+                row_sums[comp * planes + m, pl.ds(k // 4, 8, stride=depth // 4), :] = (
+                    (quad[0] + quad[1]) + (quad[2] + quad[3]))
+        return carry
+
+    lax.fori_loop(0, PAIR, filter_field, 0)
 
     side_rows = rows // 4
     edge = HALO // 4
     scale = KAPPA ** PASSES / 16.0
     for comp in range(PAIR):
-        x = jnp.concatenate([row_sums[comp * strips + s] for s in range(strips)], axis=1)
+        x = jnp.concatenate([row_sums[comp * planes + s] for s in range(planes)], axis=1)
         high = x.astype(jnp.bfloat16)
         rest = x - high.astype(jnp.float32)
         mid = rest.astype(jnp.bfloat16)
@@ -369,7 +384,7 @@
     grid_x, grid_y = ocean_mask.shape
     count = grid_x * grid_y
     slots = count // n_tile
-    strips = cols // LANES + 1
+    planes = cols // LANES + 1
     height = rows + 2 * HALO
     side_rows = rows // 4
     cells = (side_rows // grid_x) ** 2
@@ -390,11 +405,12 @@
             pltpu.SMEM(ocean_mask.shape, jnp.int32),
             pltpu.SMEM(tile_owner.shape, jnp.int32),
             pltpu.SMEM(lower_edge_quarter_turns.shape, jnp.int32),
-            pltpu.VMEM((PAIR * strips, height, LANES), f32),
-            pltpu.VMEM((height + 16, LANES), f32),
-            pltpu.VMEM((height + 16, LANES), f32),
-            pltpu.VMEM((strips * LANES, 2 * LANES), jnp.bfloat16),
-            pltpu.VMEM((PAIR * strips, height // 4, LANES), f32),
+            pltpu.VMEM((PAIR * planes, height, LANES), f32),
+            pltpu.VMEM((planes, height + 16, LANES), f32),
+            pltpu.VMEM((planes, height + 16, LANES), f32),
+            pltpu.VMEM((planes * LANES, planes * LANES), jnp.bfloat16),
+            pltpu.VMEM((planes * LANES, 2 * LANES), jnp.bfloat16),
+            pltpu.VMEM((PAIR * planes, height // 4, LANES), f32),
             pltpu.VMEM((PAIR, height // 4, LANES), f32),
             pltpu.VMEM((PAIR, height // 4, LANES), f32),
             pltpu.VMEM((5, side_rows, LANES), f32),

time: 44.9 us -> 35.5 us (0.79)
  Pallas kernels: 41.1 us -> 31.8 us
    pallas_call x1, Pallas kernels: 41.1 us -> 31.8 us  [per_device(): pl.pallas_call(functools.partial(kernel, n_tile, n_col, grid_x, grid_y),...]
where the time goes in v3:
time: 35.5 us; the launch traced here: 35.3 us
  Pallas kernels  31.8 us (90%)
  local copies, waits for them, and re-layouts  2.91 us (8%)
  between operations  0.65 us (2%)
    pallas_call x1, Pallas kernels, per_device(): pl.pallas_call(functools.partial(kernel, n_tile, n_col, grid_x, grid_y),...  31.8 us
    unnamed x4, local copies, waits for them, and re-layouts  2.91 us

profile of v3, /device:TPU:0, one launch (start us, length us, event | category | flops | bytes accessed | tf_op | source)
XLA Modules:
  0.0 35.3 jit_solution(16089800738262701700)
XLA Ops:
  0.6 31.8 %shard_map.68 = (f32[1,1,16,16,1024]{4,3,2,1,0:T(8,128)}, f32[16,16]{1,0:T(8,128)}) custom-call(f32[512,512]{1,0:T(8,128)} %u_hbm.1, f32[512,512]{1,0:T(8,128)} %v_hbm.1, s32[4,4]{1,0:T(4,128)} %mask_hbm.1, s32[4,4]{1,0:T(4,128)} %owner_hbm.1, s32[8]{0:T(128)} %turns_hbm.1), custom_call_target="tpu_custom_call" | custom-call | tf_op jit(solution)/shard_map/pallas_call | solution.py:394
  32.4 0.0 copy-start
  32.4 2.3 %copy.9 = f32[1,1,16,16,1024]{4,3,2,1,0:T(8,128)} copy(f32[1,1,16,16,1024]{4,3,2,1,0:T(8,128)} %get-tuple-element.4) | data formatting | bytes 2097152
  34.7 0.0 copy-done
  34.7 0.6 %copy.10 = f32[16,16]{1,0:T(8,128)} copy(f32[16,16]{1,0:T(8,128)S(1)} %copy-done) | data formatting | bytes 2048
Async XLA Ops:
  32.4 2.3 %copy-start = (f32[16,16]{1,0:T(8,128)S(1)}, f32[16,16]{1,0:T(8,128)}, u32[]{:S(2)}) copy-start(f32[16,16]{1,0:T(8,128)} %get-tuple-element.5) | copy-start | bytes 3076

commit v4 on v3

--- a/solution.py
+++ b/solution.py
@@ -149,12 +149,12 @@
     def exact_dot(x, w):
         high = x.astype(jnp.bfloat16)
         low = (x - high.astype(jnp.float32)).astype(jnp.bfloat16)
-        return (jnp.dot(low, w, preferred_element_type=jnp.float32)
-                + jnp.dot(high, w, preferred_element_type=jnp.float32))
+        both = jnp.dot(jnp.concatenate([high, low], axis=0), w, preferred_element_type=jnp.float32)
+        return both[:x.shape[0]] + both[x.shape[0]:]
 
     top = HALO
     chunk = 32
-    part_rows = 128
+    part_rows = 256
 
     def spread_rows(i, carry):
         comp, r = i // (rows // part_rows), (i % (rows // part_rows)) * part_rows
@@ -182,23 +182,27 @@
             shift = (HALO * (1 - j)) % LANES
             after = pltpu.roll(after, shift, 1) if shift else after
             rims.append(rim(before, after, group))
-        for j in range(0, 8, 2):
-            y = exact_dot(jnp.concatenate(rims[j:j + 2], axis=0), spread[cols:, :])
+        for j in range(0, 8, 4):
+            y = exact_dot(jnp.concatenate(rims[j:j + 4], axis=0), spread[cols:, :])
             for m in range(planes):
-                at = slice(top + j * group, top + (j + 2) * group)
+                at = slice(top + j * group, top + (j + 4) * group)
                 mixed[comp * planes + m, at, :] += y[:, m * LANES:(m + 1) * LANES]
 
     k_top = turns_ref[t]
     k_bottom = (4 - turns_ref[down]) & 3
-    for side, turns, at in ((0, k_top, 0), (1, k_bottom, top + rows)):
+    halo_rows = []
+    for side, turns in ((0, k_top), (1, k_bottom)):
         pair = turn(in_rows[side, 0], in_rows[side, 1], turns)
         before = turn(in_corners[2 * side, 0], in_corners[2 * side, 1], turns)
         after = turn(in_corners[2 * side + 1, 0], in_corners[2 * side + 1, 1], turns)
         for comp in range(PAIR):
             ends = rim(pltpu.roll(before[comp], HALO, 1), pltpu.roll(after[comp], HALO, 1), HALO)
-            y = exact_dot(jnp.concatenate([pair[comp], ends], axis=1), spread[...])
-            for m in range(planes):
-                mixed[comp * planes + m, at:at + HALO, :] = y[:, m * LANES:(m + 1) * LANES]
+            halo_rows.append(jnp.concatenate([pair[comp], ends], axis=1))
+    y = exact_dot(jnp.concatenate(halo_rows, axis=0), spread[...])
+    for k in range(2 * PAIR):
+        at = (k // PAIR) * (top + rows)
+        for m in range(planes):
+            mixed[(k % PAIR) * planes + m, at:at + HALO, :] = y[k * HALO:(k + 1) * HALO, m * LANES:(m + 1) * LANES]
 
     depth = (rows + 2 * HALO) // 8
 
@@ -249,18 +253,20 @@
     side_rows = rows // 4
     edge = HALO // 4
     scale = KAPPA ** PASSES / 16.0
+    x = jnp.concatenate([
+        jnp.concatenate([row_sums[comp * planes + m] for m in range(planes)], axis=1)
+        for comp in range(PAIR)], axis=0)
+    high = x.astype(jnp.bfloat16)
+    rest = x - high.astype(jnp.float32)
+    mid = rest.astype(jnp.bfloat16)
+    low = (rest - mid.astype(jnp.float32)).astype(jnp.bfloat16)
+    z = jnp.dot(jnp.concatenate([low, mid, high], axis=0), weights[...], preferred_element_type=jnp.float32)
+    tall = x.shape[0]
+    z = (z[:tall] + z[tall:2 * tall]) + z[2 * tall:]
     for comp in range(PAIR):
-        x = jnp.concatenate([row_sums[comp * planes + s] for s in range(planes)], axis=1)
-        high = x.astype(jnp.bfloat16)
-        rest = x - high.astype(jnp.float32)
-        mid = rest.astype(jnp.bfloat16)
-        low = (rest - mid.astype(jnp.float32)).astype(jnp.bfloat16)
-        w = weights[...]
-        z = (jnp.dot(low, w, preferred_element_type=jnp.float32)
-             + jnp.dot(mid, w, preferred_element_type=jnp.float32)
-             + jnp.dot(high, w, preferred_element_type=jnp.float32))
-        centre[comp] = z[:, :LANES] * scale
-        across[comp] = z[:, LANES:] * (0.5 * scale)
+        here = z[comp * (tall // PAIR):(comp + 1) * (tall // PAIR)]
+        centre[comp] = here[:, :LANES] * scale
+        across[comp] = here[:, LANES:] * (0.5 * scale)
 
     for r in range(0, side_rows, chunk):
         u_dx = across[0, edge + r:edge + r + chunk, :]

time: 35.5 us -> 34.9 us (0.983)
  Pallas kernels: 31.8 us -> 31.2 us
    pallas_call x1, Pallas kernels: 31.8 us -> 31.2 us  [per_device(): pl.pallas_call(functools.partial(kernel, n_tile, n_col, grid_x, grid_y),...]
where the time goes in v4:
time: 34.9 us; the launch traced here: 34.8 us
  Pallas kernels  31.2 us (89%)
  local copies, waits for them, and re-layouts  2.91 us (8%)
  between operations  0.65 us (2%)
    pallas_call x1, Pallas kernels, per_device(): pl.pallas_call(functools.partial(kernel, n_tile, n_col, grid_x, grid_y),...  31.2 us
    unnamed x4, local copies, waits for them, and re-layouts  2.91 us

profile of v4, /device:TPU:0, one launch (start us, length us, event | category | flops | bytes accessed | tf_op | source)
XLA Modules:
  0.0 34.8 jit_solution(1466036553526618571)
XLA Ops:
  0.6 31.2 %shard_map.68 = (f32[1,1,16,16,1024]{4,3,2,1,0:T(8,128)}, f32[16,16]{1,0:T(8,128)}) custom-call(f32[512,512]{1,0:T(8,128)} %u_hbm.1, f32[512,512]{1,0:T(8,128)} %v_hbm.1, s32[4,4]{1,0:T(4,128)} %mask_hbm.1, s32[4,4]{1,0:T(4,128)} %owner_hbm.1, s32[8]{0:T(128)} %turns_hbm.1), custom_call_target="tpu_custom_call" | custom-call | tf_op jit(solution)/shard_map/pallas_call | solution.py:400
  31.8 0.0 copy-start
  31.8 2.3 %copy.9 = f32[1,1,16,16,1024]{4,3,2,1,0:T(8,128)} copy(f32[1,1,16,16,1024]{4,3,2,1,0:T(8,128)} %get-tuple-element.4) | data formatting | bytes 2097152
  34.2 0.0 copy-done
  34.2 0.6 %copy.10 = f32[16,16]{1,0:T(8,128)} copy(f32[16,16]{1,0:T(8,128)S(1)} %copy-done) | data formatting | bytes 2048
Async XLA Ops:
  31.8 2.3 %copy-start = (f32[16,16]{1,0:T(8,128)S(1)}, f32[16,16]{1,0:T(8,128)}, u32[]{:S(2)}) copy-start(f32[16,16]{1,0:T(8,128)} %get-tuple-element.5) | copy-start | bytes 3076

commit v5 on v4

--- a/solution.py
+++ b/solution.py
@@ -35,12 +35,12 @@
 
 
 def kernel(n_tile, n_col, grid_x, grid_y, u_hbm, v_hbm, mask_hbm, owner_hbm, turns_hbm,
-           library_hbm, gram_ref, library_ref, inputs, mask_ref, owner_ref, turns_ref, mixed, field_b, field_c,
+           in_tiles, gram_ref, inputs, mask_ref, owner_ref, turns_ref, mixed, field_b, field_c,
            spread, weights, row_sums, centre, across, fields,
-           tiles, terms, products, out_tiles, in_tiles, block_terms, pack, in_cols, in_rows, in_corners,
+           tiles, terms, products, out_tiles, pack, in_cols, in_rows, in_corners,
            gram_out, gram_in, gram_out2, gram_in2, pick, kept, load_sem,
            halo_send, halo_recv, all_send, all_recv, sum_send, sum_recv, sum2_send, sum2_recv,
-           own_sem, store_sem):
+           own_sem):
     t = lax.axis_index("tile")
     c = lax.axis_index("col")
     up, down = lax.rem(t + n_tile - 1, n_tile), lax.rem(t + 1, n_tile)
@@ -341,26 +341,9 @@
         copy.start()
         first_sums.append(copy)
 
-    def library_step(q, carry):
-        base = in_tiles[q // slots, q % slots]
-        for n, value in enumerate(make_terms(*[base[f] for f in range(5)])):
-            block_terms[n * 8:(n + 1) * 8, :] = value
-        for s in range(8):
-            library_ref[q, :, s * LANES:(s + 1) * LANES] = block_terms[pl.ds(s, TERMS, stride=8), :]
-        return carry
-
     own.wait()
     for copy in sends:
         copy.wait()
-    half = count // 2
-    stores = [
-        pltpu.make_async_copy(library_ref.at[pl.ds(k * half, half)],
-                              library_hbm.at[0, 0, pl.ds(k * half, half)], store_sem.at[k])
-        for k in range(2)
-    ]
-    lax.fori_loop(0, half, library_step, 0)
-    stores[0].start()
-
     for copy in first_sums:
         copy.wait()
     part = jnp.sum(gram_in[...], axis=0)
@@ -375,14 +358,19 @@
         copy.start()
         second_sums.append(copy)
 
-    lax.fori_loop(half, count, library_step, 0)
-    stores[1].start()
     for copy in second_sums:
         copy.wait()
     gram = jnp.sum(gram_in2[...], axis=0) / (side_rows * side_rows)
     gram_ref[...] = gram[:, :TERMS]
-    for copy in stores:
-        copy.wait()
+
+
+def library_kernel(some, tiles_ref, gram_in_ref, library_ref, gram_ref, block_terms):
+    gram_ref[...] = gram_in_ref[...]
+    for q in range(some):
+        for n, value in enumerate(make_terms(*[tiles_ref[q, f] for f in range(5)])):
+            block_terms[q, n * 8:(n + 1) * 8, :] = value
+        for s in range(8):
+            library_ref[0, 0, q, :, s * LANES:(s + 1) * LANES] = block_terms[q, pl.ds(s, TERMS, stride=8), :]
 
 
 def per_device(n_tile, n_col, u_velocity, v_velocity, ocean_mask, tile_owner, lower_edge_quarter_turns):
@@ -397,16 +385,15 @@
     vmem = pl.BlockSpec(memory_space=pltpu.VMEM)
     hbm = pl.BlockSpec(memory_space=pltpu.HBM)
     f32 = jnp.float32
-    return pl.pallas_call(
+    received, gram = pl.pallas_call(
         functools.partial(kernel, n_tile, n_col, grid_x, grid_y),
         out_shape=(
-            jax.ShapeDtypeStruct((1, 1, count, TERMS, cells), f32),
+            jax.ShapeDtypeStruct((n_tile, slots, 5, 8, LANES), f32),
             jax.ShapeDtypeStruct((TERMS, TERMS), f32),
         ),
         in_specs=[hbm] * 5,
-        out_specs=(hbm, vmem),
+        out_specs=(vmem, vmem),
         scratch_shapes=[
-            pltpu.VMEM((count, TERMS, cells), f32),
             pltpu.VMEM((PAIR, cols // LANES, rows, LANES), f32),
             pltpu.SMEM(ocean_mask.shape, jnp.int32),
             pltpu.SMEM(tile_owner.shape, jnp.int32),
@@ -424,8 +411,6 @@
             pltpu.VMEM((TERMS, count, 8, LANES), f32),
             pltpu.VMEM((TERMS, TERMS * 8, LANES), f32),
             pltpu.VMEM((n_tile, slots, 5, 8, LANES), f32),
-            pltpu.VMEM((n_tile, slots, 5, 8, LANES), f32),
-            pltpu.VMEM((TERMS * 8, LANES), f32),
             pltpu.VMEM((2, PAIR, rows // 8, LANES), f32),
             pltpu.VMEM((2, PAIR, rows // 8, LANES), f32),
             pltpu.VMEM((2, PAIR, HALO, cols), f32),
@@ -446,11 +431,29 @@
             pltpu.SemaphoreType.DMA((n_col,)),
             pltpu.SemaphoreType.DMA((n_col,)),
             pltpu.SemaphoreType.DMA,
-            pltpu.SemaphoreType.DMA((2,)),
         ],
         compiler_params=pltpu.CompilerParams(
             collective_id=0, has_side_effects=True, vmem_limit_bytes=60 * 1024 * 1024),
     )(u_velocity, v_velocity, ocean_mask, tile_owner, lower_edge_quarter_turns)
+    some = count // 4
+    return pl.pallas_call(
+        functools.partial(library_kernel, some),
+        grid=(4,),
+        out_shape=(
+            jax.ShapeDtypeStruct((1, 1, count, TERMS, cells), f32),
+            jax.ShapeDtypeStruct((TERMS, TERMS), f32),
+        ),
+        in_specs=[
+            pl.BlockSpec((some, 5, 8, LANES), lambda i: (i, 0, 0, 0)),
+            pl.BlockSpec((TERMS, TERMS), lambda i: (0, 0)),
+        ],
+        out_specs=(
+            pl.BlockSpec((1, 1, some, TERMS, cells), lambda i: (0, 0, i, 0, 0)),
+            pl.BlockSpec((TERMS, TERMS), lambda i: (0, 0)),
+        ),
+        scratch_shapes=[pltpu.VMEM((some, TERMS * 8, LANES), f32)],
+        compiler_params=pltpu.CompilerParams(vmem_limit_bytes=60 * 1024 * 1024),
+    )(received.reshape(count, 5, 8, LANES), gram)
 
 
 def solution(mesh):

time: 34.9 us -> 35.5 us (1.017)
  Pallas kernels: 31.2 us -> 34.6 us
  local copies, waits for them, and re-layouts: 2.91 us -> 0 us
    pallas_call x0 -> x1, Pallas kernels: none -> 3.33 us  [per_device(): pl.pallas_call(functools.partial(library_kernel, some), grid=(4,), out_sh...]
    unnamed x4 -> x0, local copies, waits for them, and re-layouts: 2.91 us -> none
where the time goes in v5:
time: 35.5 us; the launch traced here: 35.3 us
  Pallas kernels  34.6 us (97%)
  between operations  0.64 us (2%)
    pallas_call x1, Pallas kernels, per_device(): pl.pallas_call(functools.partial(kernel, n_tile, n_col, grid_x, grid_y),...  31.3 us
    pallas_call x1, Pallas kernels, per_device(): pl.pallas_call(functools.partial(library_kernel, some), grid=(4,), out_sh...  3.33 us

profile of v5, /device:TPU:0, one launch (start us, length us, event | category | flops | bytes accessed | tf_op | source)
XLA Modules:
  0.0 35.3 jit_solution(4888030528351732906)
XLA Ops:
  0.6 31.3 %shard_map.68 = (f32[8,2,5,8,128]{4,3,2,1,0:T(8,128)}, f32[16,16]{1,0:T(8,128)}) custom-call(f32[512,512]{1,0:T(8,128)} %u_hbm.1, f32[512,512]{1,0:T(8,128)} %v_hbm.1, s32[4,4]{1,0:T(4,128)} %mask_hbm.1, s32[4,4]{1,0:T(4,128)} %owner_hbm.1, s32[8]{0:T(128)} %turns_hbm.1), custom_call_target="tpu_custom_call" | custom-call | tf_op jit(solution)/shard_map/pallas_call | solution.py:388
  31.9 3.3 %shard_map.69 = (f32[1,1,16,16,1024]{4,3,2,1,0:T(8,128)}, f32[16,16]{1,0:T(8,128)}) custom-call(f32[16,5,8,128]{3,2,1,0:T(8,128)} %bitcast.1, f32[16,16]{1,0:T(8,128)} %get-tuple-element.5.gram_in_ref), custom_call_target="tpu_custom_call" | custom-call | tf_op jit(solution)/shard_map/pallas_call | solution.py:439
